TPU v7x, 32 devices: a whole 2x2x4 slice. The times are simulated.
32 devices in a mesh: grp: 2 (over y), yz: 4 (over z), gx: 4 (over x, core).
Axes of the slice: x: 2, y: 2, z: 4, core: 2. Of those that a mesh axis runs over, the one named last changes fastest.
Arguments:
- hidden: bfloat16 [32, 3, 8192], P(('grp', 'yz', 'gx')), parts along dimension 0, may hold values from -3 to 3
- cache_lengths: int32 [32], P(('grp', 'yz', 'gx')), parts along dimension 0, may hold values from 1 to 256, as said below
- image_counts: int32 [32], P(('grp', 'yz', 'gx')), parts along dimension 0, may hold values from 96 to 384, as said below
- self_keys: bfloat16 [32, 256, 1024], P(('grp', 'yz', 'gx')), parts along dimension 0, may hold values from -6 to 6
- self_values: bfloat16 [32, 256, 1024], P(('grp', 'yz', 'gx')), parts along dimension 0, may hold values from -6 to 6
- image_keys: bfloat16 [32, 384, 1024], P(('grp', 'yz', 'gx')), parts along dimension 0, may hold values from -6 to 6
- image_values: bfloat16 [32, 384, 1024], P(('grp', 'yz', 'gx')), parts along dimension 0, may hold values from -6 to 6
- norm_gain: float32 [8192], replicated, may hold values from 0.1 to 1.9
- query_weight: bfloat16 [8192, 8192], P('gx', 'yz'), may hold values from -40 to 40
- kv_weight: bfloat16 [8192, 2048], P('gx', 'yz'), may hold values from -0.0625 to 0.0625
- out_weight: bfloat16 [8192, 8192], P('gx', 'yz'), may hold values from -0.0625 to 0.0625
- cross_norm_gain: float32 [8192], replicated, may hold values from 0.1 to 1.9
- cross_query_weight: bfloat16 [8192, 8192], P('gx', 'yz'), may hold values from -0.0625 to 0.0625
- query_gain: float32 [128], replicated, may hold values from 0.1 to 160
- cross_out_weight: bfloat16 [8192, 8192], P('gx', 'yz'), may hold values from -0.0625 to 0.0625
- cross_gate: float32 [1], replicated, may hold values from 0.2 to 2
Outputs:
- layer_out: bfloat16 [32, 3, 8192], P(('grp', 'yz', 'gx')), parts along dimension 0
There are 2 independent parts, one for each index of `grp`. A program takes and returns all parts, laid end to end along the dimension named above; an argument that names none is the same for every part. Nothing has to cross between parts.
Inputs may be any that keep to these rules, and one draw needn't show every extreme that they name: `cache_lengths`: some request has exactly 256 valid cached positions. `image_counts`: some request has exactly 384 image tokens.
All inputs are finite; a program needn't handle non-finite values.
Results may differ from a plain program's by a relative error of at most 0.0075.
The roundings to bfloat16 on the way count: a program that leaves them out, or rounds other values in their place, can miss the bound.
Values may be sent and summed in bfloat16 or wider, within the bound.
A program may use at most 128 MiB of HBM per device.

v0:
```python
import jax
import jax.numpy as jnp
from jax import lax
from jax.sharding import PartitionSpec as P

HEADS = 64
KV_HEADS = 8
HEAD_DIM = 128


def rms_scale(values, gain):
    return values * lax.rsqrt(jnp.mean(values * values, axis=-1, keepdims=True) + 1e-05) * gain


def rotate(values, positions):
    half_dim = values.shape[-1] // 2
    freqs = 500000.0 ** (-2.0 * jnp.arange(half_dim, dtype=jnp.float32) / values.shape[-1])
    angles = positions.astype(jnp.float32)[:, :, None, None] * freqs
    cosine = jnp.cos(angles)
    sine = jnp.sin(angles)
    first = values[..., :half_dim]
    second = values[..., half_dim:]
    return jnp.concatenate(
        [first * cosine - second * sine, second * cosine + first * sine], axis=-1
    )


def head_scores(queries, keys, valid):
    requests, drafts = (queries.shape[0], queries.shape[1])
    grouped = queries.reshape(requests, drafts, KV_HEADS, HEADS // KV_HEADS, HEAD_DIM)
    scores = jnp.einsum(
        "rskgd,rtkd->rkgst", grouped, keys, preferred_element_type=jnp.float32
    ) * HEAD_DIM ** (-0.5)
    return jnp.where(valid[:, None, None, :, :], scores, -jnp.inf)


def normalize_scores(scores):
    highest = jnp.max(scores, axis=-1, keepdims=True)
    weights = jnp.exp(scores - highest)
    return (weights / jnp.sum(weights, axis=-1, keepdims=True)).astype(jnp.bfloat16)


def order_by_group(terms):
    rank_count = lax.axis_size("yz")
    group_count = lax.axis_size("gx")
    own_reqs = terms.shape[0] // (rank_count * group_count)
    shaped = terms.reshape(rank_count, group_count, own_reqs, terms.shape[1], terms.shape[2])
    return jnp.swapaxes(shaped, 0, 1).reshape(terms.shape)


def route_features(values):
    return lax.all_to_all(values, "gx", split_axis=2, concat_axis=0, tiled=True)


def project_rows(routed, weights):
    piece = lax.all_gather(routed, "yz", axis=0, tiled=True)
    return jnp.concatenate(
        [
            jnp.einsum("rsd,dc->rsc", piece, matrix, preferred_element_type=jnp.float32)
            for matrix in weights
        ],
        axis=2,
    )


def heads_to_requests(terms):
    summed = lax.psum_scatter(order_by_group(terms), "gx", scatter_dimension=0, tiled=True).astype(
        jnp.bfloat16
    )
    return lax.all_to_all(summed, "yz", split_axis=0, concat_axis=2, tiled=True)


def rows_out(attended, weight):
    blocks = lax.all_to_all(attended, "gx", split_axis=2, concat_axis=0, tiled=True)
    terms = jnp.einsum(
        "rsc,cd->rsd",
        lax.all_gather(blocks, "yz", axis=0, tiled=True),
        weight,
        preferred_element_type=jnp.float32,
    )
    summed = lax.psum_scatter(order_by_group(terms), "gx", scatter_dimension=0, tiled=True)
    return lax.all_to_all(summed, "yz", split_axis=0, concat_axis=2, tiled=True)


def shards(
    hidden,
    cache_lengths,
    image_counts,
    self_keys,
    self_values,
    image_keys,
    image_values,
    norm_gain,
    query_weight,
    kv_weight,
    out_weight,
    cross_norm_gain,
    cross_query_weight,
    query_gain,
    cross_out_weight,
    cross_gate,
):
    own_reqs, drafts = (hidden.shape[0], hidden.shape[1])
    rank_count = lax.axis_size("yz")
    query_cols = query_weight.shape[1]
    normed = rms_scale(hidden.astype(jnp.float32), norm_gain).astype(jnp.bfloat16)
    routed = route_features(normed)
    query_terms = project_rows(routed, (query_weight,))
    kv_terms = jnp.einsum(
        "rsd,dc->rsc",
        lax.all_gather(routed, "yz", axis=0, tiled=True),
        kv_weight,
        preferred_element_type=jnp.float32,
    )
    terms = jnp.concatenate([query_terms, kv_terms], axis=2)
    received = heads_to_requests(terms).reshape(own_reqs, drafts, rank_count, terms.shape[2])
    queries = received[..., :query_cols].reshape(own_reqs, drafts, HEADS, HEAD_DIM)
    fresh = received[..., query_cols:].reshape(own_reqs, drafts, 2, KV_HEADS, HEAD_DIM)
    positions = cache_lengths[:, None] + jnp.arange(drafts, dtype=jnp.int32)[None, :]
    rotated = rotate(queries.astype(jnp.float32), positions).astype(jnp.bfloat16)
    new_keys = rotate(fresh[:, :, 0].astype(jnp.float32), positions).astype(jnp.bfloat16)
    new_values = fresh[:, :, 1]
    stored = self_keys.shape[1]
    stored_keys = self_keys.reshape(own_reqs, stored, KV_HEADS, HEAD_DIM)
    stored_values = self_values.reshape(own_reqs, stored, KV_HEADS, HEAD_DIM)
    stored_valid = jnp.arange(stored, dtype=jnp.int32)[None, None, :] < cache_lengths[:, None, None]
    stored_valid = jnp.broadcast_to(stored_valid, (own_reqs, drafts, stored))
    causal = (
        jnp.arange(drafts, dtype=jnp.int32)[None, :] <= jnp.arange(drafts, dtype=jnp.int32)[:, None]
    )
    causal = causal[None]
    scores = jnp.concatenate(
        [head_scores(rotated, stored_keys, stored_valid), head_scores(rotated, new_keys, causal)],
        axis=-1,
    )
    probs = normalize_scores(scores)
    mixed = jnp.einsum(
        "rkgst,rtkd->rskgd", probs[..., :stored], stored_values, preferred_element_type=jnp.float32
    )
    mixed = mixed + jnp.einsum(
        "rkgst,rtkd->rskgd", probs[..., stored:], new_values, preferred_element_type=jnp.float32
    )
    attended = mixed.astype(jnp.bfloat16).reshape(own_reqs, drafts, HEADS * HEAD_DIM)
    middle = (hidden.astype(jnp.float32) + rows_out(attended, out_weight)).astype(jnp.bfloat16)
    cross_normed = rms_scale(middle.astype(jnp.float32), cross_norm_gain).astype(jnp.bfloat16)
    cross_routed = route_features(cross_normed)
    cross_terms = project_rows(cross_routed, (cross_query_weight,))
    cross_queries = heads_to_requests(cross_terms).reshape(own_reqs, drafts, HEADS, HEAD_DIM)
    normed_queries = rms_scale(cross_queries.astype(jnp.float32), query_gain).astype(jnp.bfloat16)
    slots = image_keys.shape[1]
    image_valid = jnp.arange(slots, dtype=jnp.int32)[None, None, :] < image_counts[:, None, None]
    image_valid = jnp.broadcast_to(image_valid, (own_reqs, drafts, slots))
    cross_probs = normalize_scores(
        head_scores(
            normed_queries, image_keys.reshape(own_reqs, slots, KV_HEADS, HEAD_DIM), image_valid
        )
    )
    cross_mixed = jnp.einsum(
        "rkgst,rtkd->rskgd",
        cross_probs,
        image_values.reshape(own_reqs, slots, KV_HEADS, HEAD_DIM),
        preferred_element_type=jnp.float32,
    )
    cross_attended = cross_mixed.astype(jnp.bfloat16).reshape(own_reqs, drafts, HEADS * HEAD_DIM)
    cross_projected = rows_out(cross_attended, cross_out_weight)
    layer_out = middle.astype(jnp.float32) + jnp.tanh(cross_gate[0]) * cross_projected
    return layer_out.astype(jnp.bfloat16)


def solution(mesh):
    placed = (
        P(("grp", "yz", "gx"), None, None),
        P(("grp", "yz", "gx")),
        P(("grp", "yz", "gx")),
        P(("grp", "yz", "gx"), None, None),
        P(("grp", "yz", "gx"), None, None),
        P(("grp", "yz", "gx"), None, None),
        P(("grp", "yz", "gx"), None, None),
        P(),
        P("gx", "yz"),
        P("gx", "yz"),
        P("gx", "yz"),
        P(),
        P("gx", "yz"),
        P(),
        P("gx", "yz"),
        P(),
    )
    return jax.shard_map(
        shards,
        mesh=mesh,
        in_specs=placed,
        out_specs=P(("grp", "yz", "gx"), None, None),
        check_vma=False,
    )
```

profile of v0, /device:TPU:0, one launch (start us, length us, event | category | flops | bytes accessed | tf_op | source)
XLA Modules:
  0.0 545.6 jit_solution(1199618045679000272)
XLA Ops:
  6.5 1.2 multiply_reduce_fusion.1
  7.8 1.0 multiply_convert_fusion.2
  8.8 6.9 %copy.210 = bf16[1,3,8192]{1,0,2:T(2,128)(2,1)} copy(bf16[1,3,8192]{2,0,1:T(2,128)(2,1)S(1)} %multiply_convert_fusion.2) | data formatting | bytes 98304 | tf_op jit(solution)/shard_map/convert_element_type | solution.py:106
  15.7 0.5 broadcast.226
  16.2 46.5 %reduce.11 = bf16[8192,3]{1,0:T(8,128)(2,1)} reduce(bf16[8192,1,3]{2,1,0:T(2,128)(2,1)} %bitcast.198, bf16[]{:T(256)} %broadcast.226), dimensions={1}, to_apply=%bitcast.180.reduce_sub_computation | reduce | bytes 98306
  62.7 4.7 reshape.522
  67.3 4.2 all-to-all-start
  72.4 1.1 copy.281
  73.6 0.6 dynamic-slice
  74.8 0.7 all-to-all-done
  75.6 5.3 reshape.523
  80.9 8.1 %copy.211 = bf16[1,3,8192]{2,1,0:T(4,128)(2,1)S(1)} copy(bf16[1,3,8192]{1,0,2:T(2,128)(2,1)} %bitcast.200) | data formatting | bytes 98304 | tf_op jit(solution)/shard_map/all_to_all | solution.py:52
  89.1 14.6 %all-gather = bf16[16,1,3,2048]{3,2,1,0:T(4,128)(2,1)S(1)} all-gather(bf16[4,1,3,2048]{3,2,1,0:T(4,128)(2,1)S(1)} %copy.212), channel_id=2, replica_groups=mesh['grp'=2,'yz'=4,'gx'=4] {'yz'}, dimensions={0}, use_global_device_ids=true | all-gather | bytes 245760 | tf_op jit(solution)/shard_map/all_gather | solution.py:56
  103.8 5.0 fusion.6
  108.8 0.5 fusion.8
  109.8 15.6 %all-reduce.12 = bf16[16,3,2560]{2,0,1:T(8,128)(2,1)S(1)} all-reduce(f32[16,3,2560]{2,0,1:T(8,128)S(1)} %reshape.473), channel_id=6, replica_groups=mesh['grp'=2,'yz'=4,'gx'=4] {'gx'}, use_global_device_ids=true, to_apply=%region_1.0.clone | all-reduce | flops 122880 | bytes 737280
  125.5 0.7 copy.215
  126.1 5.2 all-to-all-start.1
  131.4 5.8 %all-to-all-done.1 = bf16[4,3,2560]{2,1,0:T(4,128)(2,1)S(1)} async-done(((bf16[4,3,2560]{2,1,0:T(4,128)(2,1)}), bf16[4,3,2560]{2,1,0:T(4,128)(2,1)S(1)}, u32[]{:S(2)}, u32[]{:S(2)}) %all-to-all-start.1) | async-done | bytes 61472 | tf_op jit(solution)/shard_map/all_to_all | solution.py:70
  137.5 0.4 fusion.55
  137.9 0.3 fusion.56
  138.9 6.8 %copy.226 = bf16[1,3,8192]{1,0,2:T(2,128)(2,1)} copy(bf16[1,3,8192]{2,1,0:T(4,128)(2,1)S(1)} %reshape.480) | data formatting | bytes 98304 | tf_op jit(solution)/shard_map/reshape | solution.py:143
  145.8 45.1 %reduce.12 = bf16[8192,3]{1,0:T(8,128)(2,1)S(1)} reduce(bf16[8192,1,3]{2,1,0:T(2,128)(2,1)} %bitcast.201, bf16[]{:T(256)} %broadcast.226), dimensions={1}, to_apply=%bitcast.182.reduce_sub_computation | reduce | bytes 98306
  190.9 3.1 reshape.524
  194.0 6.4 %all_to_all.123 = bf16[4,2,3072]{2,1,0:T(2,128)(2,1)S(1)} all-to-all(bf16[4,2,3072]{2,1,0:T(2,128)(2,1)S(1)} %reshape.524), channel_id=1, replica_groups=mesh['grp'=2,'yz'=4,'gx'=4] {'gx'}, dimensions={0} | all-to-all | bytes 98304 | tf_op jit(solution)/shard_map/all_to_all | solution.py:74
  200.4 5.3 reshape.525
  205.7 8.1 %copy.227 = bf16[1,3,8192]{2,1,0:T(4,128)(2,1)S(1)} copy(bf16[1,3,8192]{1,0,2:T(2,128)(2,1)} %bitcast.202) | data formatting | bytes 98304 | tf_op jit(solution)/shard_map/all_to_all | solution.py:74
  214.0 14.6 %all-gather.1 = bf16[16,1,3,2048]{3,2,1,0:T(4,128)(2,1)S(1)} all-gather(bf16[4,1,3,2048]{3,2,1,0:T(4,128)(2,1)S(1)} %copy.228), channel_id=3, replica_groups=mesh['grp'=2,'yz'=4,'gx'=4] {'yz'}, dimensions={0}, use_global_device_ids=true | all-gather | bytes 245760 | tf_op jit(solution)/shard_map/all_gather | solution.py:77
  228.5 5.0 fusion.4
  233.9 0.9 reshape.482
  234.8 30.1 %all-reduce.9.cloned.1.call-done = f32[16,3,2048]{2,0,1:T(8,128)} async-done(((f32[16,3,2048]{2,0,1:T(8,128)}), f32[16,3,2048]{2,0,1:T(8,128)}) %all-reduce.9.cloned.1.call-update) | async-done | bytes 393232
  264.9 0.9 constant_dynamic-slice_fusion.1
  265.9 10.7 %all_to_all.124 = f32[4,3,2048]{2,1,0:T(4,128)S(1)} all-to-all(f32[4,3,2048]{2,1,0:T(4,128)S(1)} %copy.231), channel_id=1, replica_groups=mesh['grp'=2,'yz'=4,'gx'=4] {'yz'}, dimensions={0} | all-to-all | bytes 196608 | tf_op jit(solution)/shard_map/all_to_all | solution.py:82
  277.3 6.9 %copy.233 = bf16[1,3,8192]{1,0,2:T(2,128)(2,1)} copy(bf16[1,3,8192]{2,0,1:T(2,128)(2,1)S(1)} %multiply_convert_fusion.1) | data formatting | bytes 98304 | tf_op jit(solution)/shard_map/convert_element_type | solution.py:145
  284.2 45.1 %reduce.13 = bf16[8192,3]{1,0:T(8,128)(2,1)S(1)} reduce(bf16[8192,1,3]{2,1,0:T(2,128)(2,1)} %bitcast.203, bf16[]{:T(256)} %broadcast.226), dimensions={1}, to_apply=%bitcast.184.reduce_sub_computation | reduce | bytes 98306
  329.3 3.7 reshape.526
  333.0 3.3 all-to-all-start.4
  337.1 1.3 copy.283
  338.4 1.8 all-to-all-done.4
  340.2 5.3 reshape.527
  345.6 8.1 %copy.234 = bf16[1,3,8192]{2,1,0:T(4,128)(2,1)S(1)} copy(bf16[1,3,8192]{1,0,2:T(2,128)(2,1)} %bitcast.204) | data formatting | bytes 98304 | tf_op jit(solution)/shard_map/all_to_all | solution.py:52
  353.8 14.4 %all-gather.2 = bf16[16,1,3,2048]{3,2,1,0:T(4,128)(2,1)S(1)} all-gather(bf16[4,1,3,2048]{3,2,1,0:T(4,128)(2,1)S(1)} %copy.235), channel_id=4, replica_groups=mesh['grp'=2,'yz'=4,'gx'=4] {'yz'}, dimensions={0}, use_global_device_ids=true | all-gather | bytes 245760 | tf_op jit(solution)/shard_map/all_gather | solution.py:56
  368.2 5.0 fusion.2
  373.7 14.5 %all-reduce.13 = bf16[16,3,2048]{2,0,1:T(8,128)(2,1)S(1)} all-reduce(f32[16,3,2048]{2,0,1:T(8,128)S(1)} %reshape.484), channel_id=8, replica_groups=mesh['grp'=2,'yz'=4,'gx'=4] {'gx'}, use_global_device_ids=true, to_apply=%region_7.8.clone | all-reduce | flops 98304 | bytes 589824
  388.2 0.7 copy.238
  388.9 3.3 all-to-all-start.5
  392.4 5.5 %all-to-all-done.5 = bf16[4,3,2048]{2,1,0:T(4,128)(2,1)S(1)} async-done(((bf16[4,3,2048]{2,1,0:T(4,128)(2,1)}), bf16[4,3,2048]{2,1,0:T(4,128)(2,1)S(1)}, u32[]{:S(2)}, u32[]{:S(2)}) %all-to-all-start.5) | async-done | bytes 49184 | tf_op jit(solution)/shard_map/all_to_all | solution.py:70
  398.4 0.5 fusion.57
  399.1 0.3 fusion.19
  399.5 6.8 %copy.245 = bf16[1,3,8192]{1,0,2:T(2,128)(2,1)} copy(bf16[1,3,8192]{2,1,0:T(4,128)(2,1)S(1)} %reshape.488) | data formatting | bytes 98304 | tf_op jit(solution)/shard_map/reshape | solution.py:164
  406.4 45.1 %reduce.14 = bf16[8192,3]{1,0:T(8,128)(2,1)S(1)} reduce(bf16[8192,1,3]{2,1,0:T(2,128)(2,1)} %bitcast.199, bf16[]{:T(256)} %broadcast.226), dimensions={1}, to_apply=%bitcast.186.reduce_sub_computation | reduce | bytes 98306
  451.5 3.1 reshape.528
  454.6 6.4 %all_to_all.125 = bf16[4,2,3072]{2,1,0:T(2,128)(2,1)S(1)} all-to-all(bf16[4,2,3072]{2,1,0:T(2,128)(2,1)S(1)} %reshape.528), channel_id=1, replica_groups=mesh['grp'=2,'yz'=4,'gx'=4] {'gx'}, dimensions={0} | all-to-all | bytes 98304 | tf_op jit(solution)/shard_map/all_to_all | solution.py:74
  461.0 5.3 reshape.529
  466.3 8.2 %copy.246 = bf16[1,3,8192]{2,1,0:T(4,128)(2,1)S(1)} copy(bf16[1,3,8192]{1,0,2:T(2,128)(2,1)} %bitcast.205) | data formatting | bytes 98304 | tf_op jit(solution)/shard_map/all_to_all | solution.py:74
  474.7 14.3 %all-gather.3 = bf16[16,1,3,2048]{3,2,1,0:T(4,128)(2,1)S(1)} all-gather(bf16[4,1,3,2048]{3,2,1,0:T(4,128)(2,1)S(1)} %copy.247), channel_id=5, replica_groups=mesh['grp'=2,'yz'=4,'gx'=4] {'yz'}, dimensions={0}, use_global_device_ids=true | all-gather | bytes 245760 | tf_op jit(solution)/shard_map/all_gather | solution.py:77
  489.0 5.0 fusion
  494.4 0.9 reshape.490
  495.3 30.1 %all-reduce.11.cloned.1.call-done = f32[16,3,2048]{2,0,1:T(8,128)} async-done(((f32[16,3,2048]{2,0,1:T(8,128)}), f32[16,3,2048]{2,0,1:T(8,128)}) %all-reduce.11.cloned.1.call-update) | async-done | bytes 393232
  525.4 0.9 constant_dynamic-slice_fusion
  526.3 0.7 copy.250
  527.0 4.6 all-to-all-start.7
  532.3 5.2 all-to-all-done.7
  537.9 0.7 copy.252
  (88 shorter events, 5.8 us)
Async XLA Ops:
  6.5 102.2 %copy-start = (bf16[2048,512]{1,0:T(8,128)(2,1)S(1)}, bf16[2048,512]{1,0:T(8,128)(2,1)}, u32[]{:S(2)}) copy-start(bf16[2048,512]{1,0:T(8,128)(2,1)} %param.25) | copy-start | bytes 6291460
  6.5 67.1 %copy-start.7 = (u32[32]{0:T(128)S(1)}, u32[32]{0:T(128)}, u32[]{:S(2)}) copy-start(u32[32]{0:T(128)} %constant.34) | copy-start | bytes 388
  6.5 65.8 %copy-start.4 = (bf16[1,256,1024]{2,1,0:T(8,128)(2,1)S(1)}, bf16[1,256,1024]{2,1,0:T(8,128)(2,1)}, u32[]{:S(2)}) copy-start(bf16[1,256,1024]{2,1,0:T(8,128)(2,1)} %param.19) | copy-start | bytes 1572868
  67.3 8.2 %all-to-all-start = ((bf16[4,2,3072]{2,1,0:T(2,128)(2,1)}), bf16[4,2,3072]{2,1,0:T(2,128)(2,1)S(1)}, u32[]{:S(2)}, u32[]{:S(2)}) async-start(bf16[4,2,3072]{2,1,0:T(2,128)(2,1)} %reshape.522), calls=%async_computation | async-start | bytes 98304 | tf_op jit(solution)/shard_map/all_to_all | solution.py:52
  126.1 11.0 %all-to-all-start.1 = ((bf16[4,3,2560]{2,1,0:T(4,128)(2,1)}), bf16[4,3,2560]{2,1,0:T(4,128)(2,1)S(1)}, u32[]{:S(2)}, u32[]{:S(2)}) async-start(bf16[4,3,2560]{2,1,0:T(4,128)(2,1)} %copy.215), calls=%async_computation.1 | async-start | bytes 163840 | tf_op jit(solution)/shard_map/all_to_all | solution.py:70
  131.3 133.6 %all-reduce.9.cloned.1.call-start = ((), (), s32[]{:S(2)}) async-start(), calls=%async_computation.8 | async-start | bytes 786432
  213.8 63.0 %copy-start.3 = (bf16[1,3,8192]{2,1,0:T(4,128)(2,1)S(1)}, bf16[1,3,8192]{2,1,0:T(4,128)(2,1)}, u32[]{:S(2)}) copy-start(bf16[1,3,8192]{2,1,0:T(4,128)(2,1)} %param.16) | copy-start | bytes 147460
  213.8 63.3 %copy-start.5 = (f32[8192]{0:T(1024)S(1)}, f32[8192]{0:T(1024)}, u32[]{:S(2)}) copy-start(f32[8192]{0:T(1024)} %param.27) | copy-start | bytes 98308
  233.6 102.6 %copy-start.2 = (bf16[1,384,1024]{2,1,0:T(8,128)(2,1)S(1)}, bf16[1,384,1024]{2,1,0:T(8,128)(2,1)}, u32[]{:S(2)}) copy-start(bf16[1,384,1024]{2,1,0:T(8,128)(2,1)} %param.21) | copy-start | bytes 2359300
  333.0 7.3 %all-to-all-start.4 = ((bf16[4,2,3072]{2,1,0:T(2,128)(2,1)}), bf16[4,2,3072]{2,1,0:T(2,128)(2,1)S(1)}, u32[]{:S(2)}, u32[]{:S(2)}) async-start(bf16[4,2,3072]{2,1,0:T(2,128)(2,1)} %reshape.526), calls=%async_computation.4 | async-start | bytes 98304 | tf_op jit(solution)/shard_map/all_to_all | solution.py:52
  353.8 44.7 %copy-start.6 = (f32[128]{0:T(128)S(1)}, f32[128]{0:T(128)}, u32[]{:S(2)}) copy-start(f32[128]{0:T(128)} %param.29) | copy-start | bytes 1540
  388.9 9.0 %all-to-all-start.5 = ((bf16[4,3,2048]{2,1,0:T(4,128)(2,1)}), bf16[4,3,2048]{2,1,0:T(4,128)(2,1)S(1)}, u32[]{:S(2)}, u32[]{:S(2)}) async-start(bf16[4,3,2048]{2,1,0:T(4,128)(2,1)} %copy.238), calls=%async_computation.5 | async-start | bytes 131072 | tf_op jit(solution)/shard_map/all_to_all | solution.py:70
  392.2 133.2 %all-reduce.11.cloned.1.call-start = ((), (), s32[]{:S(2)}) async-start(), calls=%async_computation.9 | async-start | bytes 786432
  466.3 72.3 %copy-start.1 = (bf16[2048,512]{1,0:T(8,128)(2,1)S(1)}, bf16[2048,512]{1,0:T(8,128)(2,1)}, u32[]{:S(2)}) copy-start(bf16[2048,512]{1,0:T(8,128)(2,1)} %param.25) | copy-start | bytes 6291460
  527.0 10.5 %all-to-all-start.7 = ((f32[4,3,2048]{2,1,0:T(4,128)}), f32[4,3,2048]{2,1,0:T(4,128)S(1)}, u32[]{:S(2)}, u32[]{:S(2)}) async-start(f32[4,3,2048]{2,1,0:T(4,128)} %copy.250), calls=%async_computation.7 | async-start | bytes 262144 | tf_op jit(solution)/shard_map/all_to_all | solution.py:82
Sparse Core Ops, SparseCore 0:
  234.9 29.9 all-reduce.8
  495.4 29.9 all-reduce.10
where the time goes:
time: 556 us; the launch traced here: 546 us
  other arithmetic  186 us (33%)
  blocking collectives  111 us (20%)
  local copies, waits for them, and re-layouts  109 us (20%)
  waiting for transfers between devices  79.3 us (14%)
  matrix products  22.2 us (4%)
  starting transfers between devices  20.8 us (4%)
  between operations  16.9 us (3%)
    unnamed x4, other arithmetic  182 us
    unnamed x4, waiting for transfers between devices  60.2 us
    unnamed x32, local copies, waits for them, and re-layouts  41.5 us
    unnamed x2, blocking collectives  30.1 us
    all_gather x2, blocking collectives, project_rows(): piece = lax.all_gather(routed, 'yz', axis=0, tiled=True)  29 us
    all_gather x2, blocking collectives, rows_out(): lax.all_gather(blocks, 'yz', axis=0, tiled=True)  28.9 us
    all_to_all x6, local copies, waits for them, and re-layouts, rows_out(): lax.all_to_all(attended, 'gx', split_axis=2, concat_axis=0, tiled=True)  16.6 us
    all_to_all x6, local copies, waits for them, and re-layouts, route_features(): return lax.all_to_all(values, 'gx', split_axis=2, concat_axis=0, tiled=True)  16.4 us
  transfers between devices with their start and end apart: 7, of which 7 were waited for; matrix products, arithmetic and copies ran while one was open for 1% of the time, Pallas kernels for 0%

commit v1 on v0

--- a/solution.py
+++ b/solution.py
@@ -1,6 +1,10 @@
+import functools
+
 import jax
 import jax.numpy as jnp
 from jax import lax
+from jax.experimental import pallas as pl
+from jax.experimental.pallas import tpu as pltpu
 from jax.sharding import PartitionSpec as P
 
 HEADS = 64
@@ -82,7 +86,7 @@
     return lax.all_to_all(summed, "yz", split_axis=0, concat_axis=2, tiled=True)
 
 
-def shards(
+def shards_by_collectives(
     hidden,
     cache_lengths,
     image_counts,
@@ -167,6 +171,486 @@
     return layer_out.astype(jnp.bfloat16)
 
 
+LANES = 128
+TILE = 16
+BF16 = jnp.bfloat16
+F32 = jnp.float32
+
+
+def layer_kernel(
+    nz,
+    nx,
+    drafts,
+    lengths_ref,
+    counts_ref,
+    gate_ref,
+    hidden_ref,
+    gain_ref,
+    cross_gain_ref,
+    query_gain_ref,
+    cos_ref,
+    sin_ref,
+    self_keys_ref,
+    self_values_ref,
+    image_keys_ref,
+    image_values_ref,
+    wq_ref,
+    wkv_ref,
+    wo_ref,
+    wcq_ref,
+    wco_ref,
+    out_ref,
+    wq,
+    wkv,
+    wo,
+    wcq,
+    wco,
+    keys,
+    values,
+    ikeys,
+    ivalues,
+    hid,
+    mid,
+    wide,
+    lhs,
+    rows_out_buf,
+    rows_in,
+    part_out,
+    part_in,
+    total,
+    tile_f,
+    tile_b,
+    route_b,
+    route_f,
+    heads_f,
+    heads_b,
+    load_sem,
+    scat_send,
+    scat_recv,
+    part_send,
+    part_recv,
+    route_send,
+    route_recv,
+):
+    n = nz * nx
+    j = lax.axis_index("yz")
+    i = lax.axis_index("gx")
+    me = j * nx + i
+    chunks = hid.shape[0] // drafts
+    block = chunks // nx
+    cols = wo.shape[1] // nx
+    per = cols // LANES
+    slots = self_keys_ref.shape[0]
+
+    def place(d):
+        return {"yz": d // nx, "gx": d % nx}
+
+    loads = [
+        (wq_ref, wq),
+        (wkv_ref, wkv),
+        (self_keys_ref, keys.at[pl.ds(0, slots)]),
+        (self_values_ref, values.at[pl.ds(0, slots)]),
+        (wo_ref, wo),
+        (wcq_ref, wcq),
+        (image_keys_ref, ikeys),
+        (image_values_ref, ivalues),
+        (wco_ref, wco),
+    ]
+    copies = [pltpu.make_async_copy(a, b, load_sem.at[k]) for k, (a, b) in enumerate(loads)]
+    copies[0].start()
+    copies[1].start()
+
+    barrier = pltpu.get_barrier_semaphore()
+
+    def greet(k, _):
+        pl.semaphore_signal(
+            barrier, inc=1, device_id=place((me + k) % n), device_id_type=pl.DeviceIdType.MESH
+        )
+        return 0
+
+    lax.fori_loop(1, n, greet, 0)
+
+    def norm_rows(rows, gain):
+        scaled = []
+        for s in range(drafts):
+            x = rows[s * chunks : (s + 1) * chunks, :]
+            mean = jnp.sum(jnp.sum(x * x, axis=0, keepdims=True), axis=1, keepdims=True) / (
+                chunks * LANES
+            )
+            scaled.append(x * lax.rsqrt(mean + 1e-05) * gain)
+        return scaled
+
+    def scatter_copy(stage, k, source, target):
+        d = (me + k) % n
+        return pltpu.make_async_remote_copy(
+            src_ref=rows_out_buf.at[stage, :, pl.ds(pl.multiple_of((source % nx) * block, block), block)],
+            dst_ref=rows_in.at[stage, target],
+            send_sem=scat_send.at[stage, k],
+            recv_sem=scat_recv.at[stage, k],
+            device_id=place(d),
+            device_id_type=pl.DeviceIdType.MESH,
+        )
+
+    def scatter(stage):
+        def send(k, _):
+            scatter_copy(stage, k, (me + k) % n, me).start()
+            return 0
+
+        lax.fori_loop(1, n, send, 0)
+
+    def gather(stage):
+        rows = drafts * block
+        own = rows_out_buf[stage, :, pl.ds(pl.multiple_of(i * block, block), block), :]
+        wide[pl.ds(pl.multiple_of(me * rows, TILE), rows), :] = own.reshape(rows, LANES).astype(F32)
+
+        def take(k, _):
+            source = (me - k + n) % n
+            scatter_copy(stage, k, me, source).wait_recv()
+            got = rows_in[stage, source]
+            wide[pl.ds(pl.multiple_of(source * rows, TILE), rows), :] = got.reshape(
+                rows, LANES
+            ).astype(F32)
+            return 0
+
+        lax.fori_loop(1, n, take, 0)
+        for s in range(drafts):
+            for c in range(block):
+                lhs[s * n : (s + 1) * n, c * LANES : (c + 1) * LANES] = wide[
+                    pl.ds(s * block + c, n, stride=rows), :
+                ].astype(BF16)
+
+    def peer(step, sign):
+        half = nx // 2
+        flip = nx - 1 - step
+        return ((i // 2 + sign * (flip // 2) + half) % half) * 2 + (i % 2 + flip % 2) % 2
+
+    def part_copy(stage, step, width, target):
+        return pltpu.make_async_remote_copy(
+            src_ref=part_out.at[stage, step, :, pl.ds(0, width)],
+            dst_ref=part_in.at[stage, step, :, pl.ds(0, width)],
+            send_sem=part_send.at[stage, step],
+            recv_sem=part_recv.at[stage, step],
+            device_id={"gx": target},
+            device_id_type=pl.DeviceIdType.MESH,
+        )
+
+    def project(stage, weights):
+        width = sum(w.shape[1] // nx for w in weights)
+
+        def piece(target):
+            return [
+                jnp.dot(
+                    lhs[...],
+                    w[:, pl.ds(pl.multiple_of(target * (w.shape[1] // nx), LANES), w.shape[1] // nx)],
+                    preferred_element_type=F32,
+                )
+                for w in weights
+            ]
+
+        def send(step, _):
+            target = peer(step, 1)
+            at = 0
+            for term in piece(target):
+                part_out[stage, step, :, at : at + term.shape[1]] = term
+                at += term.shape[1]
+            part_copy(stage, step, width, target).start()
+            return 0
+
+        lax.fori_loop(0, nx - 1, send, 0)
+        at = 0
+        for term in piece(i):
+            total[:, at : at + term.shape[1]] = term
+            at += term.shape[1]
+        for step in range(nx - 1):
+            part_copy(stage, step, width, peer(step, 1)).wait_recv()
+            total[:, :width] += part_in[stage, step, :, :width]
+        return width // LANES
+
+    def route_copy(stage, buf_out, buf_in, k, source, target):
+        return pltpu.make_async_remote_copy(
+            src_ref=buf_out.at[source],
+            dst_ref=buf_in.at[target],
+            send_sem=route_send.at[stage, k],
+            recv_sem=route_recv.at[stage, k],
+            device_id=place((me + k) % n),
+            device_id_type=pl.DeviceIdType.MESH,
+        )
+
+    def route(stage, heads, buf_out, buf_in):
+        for s in range(drafts):
+            for h in range(heads):
+                tile_f[pl.ds(s * heads + h, n, stride=TILE), :] = total[
+                    s * n : (s + 1) * n, h * LANES : (h + 1) * LANES
+                ]
+        buf_out[...] = tile_f[...].reshape(n, TILE, LANES).astype(buf_out.dtype)
+
+        def send(k, _):
+            route_copy(stage, buf_out, buf_in, k, (me + k) % n, me).start()
+            return 0
+
+        lax.fori_loop(1, n, send, 0)
+        buf_in[me] = buf_out[me]
+
+        def take(k, _):
+            route_copy(stage, buf_out, buf_in, k, me, (me - k + n) % n).wait_recv()
+            return 0
+
+        lax.fori_loop(1, n, take, 0)
+
+    def attend(stage, kref, vref, kv_heads, valid, heads):
+        tiles = n // kv_heads
+        for k in range(kv_heads):
+            q = heads_b[k * tiles * TILE : (k + 1) * tiles * TILE, :]
+            lanes = slice(k * LANES, (k + 1) * LANES)
+            scores = lax.dot_general(
+                q, kref[:, lanes], (((1,), (1,)), ((), ())), preferred_element_type=F32
+            ) * LANES ** (-0.5)
+            scores = jnp.where(valid, scores, -jnp.inf)
+            weights = jnp.exp(scores - jnp.max(scores, axis=-1, keepdims=True))
+            probs = (weights / jnp.sum(weights, axis=-1, keepdims=True)).astype(BF16)
+            heads_f[k * tiles * TILE : (k + 1) * tiles * TILE, :] = jnp.dot(
+                probs, vref[:, lanes], preferred_element_type=F32
+            )
+        for s in range(drafts):
+            for d in range(n):
+                at = s * chunks + d * per
+                wide[at : at + per, :] = heads_f[
+                    d * TILE + s * heads : d * TILE + s * heads + per, :
+                ]
+        rows_out_buf[stage] = (
+            wide[: drafts * chunks, :].reshape(drafts, chunks, LANES).astype(BF16)
+        )
+
+    for c in range(chunks):
+        hid[pl.ds(c, drafts, stride=chunks), :] = hidden_ref[
+            :, c * LANES : (c + 1) * LANES
+        ].astype(F32)
+    for s, x in enumerate(norm_rows(hid, gain_ref[...])):
+        rows_out_buf[0, s] = x.astype(BF16)
+    tile_f[...] = jnp.zeros_like(tile_f)
+    pl.semaphore_wait(barrier, n - 1)
+    scatter(0)
+    for copy in copies[2:]:
+        copy.start()
+    pad = keys.shape[0] - slots
+    keys[slots:, :] = jnp.zeros((pad, keys.shape[1]), BF16)
+    values[slots:, :] = jnp.zeros((pad, values.shape[1]), BF16)
+
+    gather(0)
+    copies[0].wait()
+    copies[1].wait()
+    heads = project(0, (wq, wkv))
+    route(0, heads, tile_b.at[0], route_b.at[0])
+    got = route_b[0].reshape(n * TILE, LANES).astype(F32)
+    cosine = jnp.concatenate([cos_ref[...]] * n, axis=0)
+    sine = jnp.concatenate([sin_ref[...]] * n, axis=0)
+    heads_b[...] = (got * cosine + pltpu.roll(got, LANES // 2, 1) * sine).astype(BF16)
+    copies[2].wait()
+    copies[3].wait()
+    kv_heads = n // 2
+    for k in range(kv_heads):
+        lanes = slice(k * LANES, (k + 1) * LANES)
+        keys[slots : slots + TILE, lanes] = heads_b[k * TILE : (k + 1) * TILE, :]
+        values[slots : slots + TILE, lanes] = route_b[0, kv_heads + k]
+    shape = (n // kv_heads * TILE, keys.shape[0])
+    row = lax.broadcasted_iota(jnp.int32, shape, 0) % TILE
+    column = lax.broadcasted_iota(jnp.int32, shape, 1)
+    valid = column < lengths_ref[0]
+    for s in range(drafts):
+        valid = valid | ((column == slots + s * heads + per) & (row >= s * heads))
+    attend(1, keys, values, kv_heads, valid, heads)
+    scatter(1)
+    gather(1)
+    copies[4].wait()
+    heads = project(1, (wo,))
+    tile_f[...] = jnp.zeros_like(tile_f)
+    route(1, heads, route_f.at[0], route_f.at[1])
+    for s in range(drafts):
+        for d in range(n):
+            at = s * chunks + d * per
+            mid[at : at + per, :] = hid[at : at + per, :] + route_f[1, d, s * per : (s + 1) * per, :]
+    mid[...] = mid[...].astype(BF16).astype(F32)
+
+    for s, x in enumerate(norm_rows(mid, cross_gain_ref[...])):
+        rows_out_buf[2, s] = x.astype(BF16)
+    scatter(2)
+    gather(2)
+    copies[5].wait()
+    heads = project(2, (wcq,))
+    route(2, heads, tile_b.at[1], route_b.at[1])
+    got = route_b[1].reshape(n * TILE, LANES).astype(F32)
+    scale = lax.rsqrt(jnp.mean(got * got, axis=-1, keepdims=True) + 1e-05)
+    heads_b[...] = (got * scale * query_gain_ref[...]).astype(BF16)
+    copies[6].wait()
+    copies[7].wait()
+    shape = (n // kv_heads * TILE, ikeys.shape[0])
+    valid = lax.broadcasted_iota(jnp.int32, shape, 1) < counts_ref[0]
+    attend(3, ikeys, ivalues, kv_heads, valid, heads)
+    scatter(3)
+    gather(3)
+    copies[8].wait()
+    heads = project(3, (wco,))
+    route(3, heads, route_f.at[2], route_f.at[3])
+    gate = jnp.tanh(jnp.full((1, LANES), gate_ref[0], F32))
+    for s in range(drafts):
+        for d in range(n):
+            at = s * chunks + d * per
+            wide[at : at + per, :] = (
+                mid[at : at + per, :] + gate * route_f[3, d, s * per : (s + 1) * per, :]
+            )
+    for c in range(chunks):
+        out_ref[:, c * LANES : (c + 1) * LANES] = wide[
+            pl.ds(c, drafts, stride=chunks), :
+        ].astype(BF16)
+
+    for stage in range(4):
+
+        def sent(k, _):
+            scatter_copy(stage, k, me, me).wait_send()
+            out_buf, in_buf = [
+                (tile_b.at[0], route_b.at[0]),
+                (route_f.at[0], route_f.at[1]),
+                (tile_b.at[1], route_b.at[1]),
+                (route_f.at[2], route_f.at[3]),
+            ][stage]
+            route_copy(stage, out_buf, in_buf, k, me, me).wait_send()
+            return 0
+
+        lax.fori_loop(1, n, sent, 0)
+        width = total.shape[1] if stage == 0 else cols
+        for step in range(nx - 1):
+            part_copy(stage, step, width, peer(step, 1)).wait_send()
+
+
+def shards_by_kernel(
+    hidden,
+    cache_lengths,
+    image_counts,
+    self_keys,
+    self_values,
+    image_keys,
+    image_values,
+    norm_gain,
+    query_weight,
+    kv_weight,
+    out_weight,
+    cross_norm_gain,
+    cross_query_weight,
+    query_gain,
+    cross_out_weight,
+    cross_gate,
+):
+    nz, nx = lax.axis_size("yz"), lax.axis_size("gx")
+    n = nz * nx
+    drafts, model = hidden.shape[1], hidden.shape[2]
+    chunks = model // LANES
+    cols = query_weight.shape[1] // nx
+    width = cols + kv_weight.shape[1] // nx
+    per = width // LANES
+    position = cache_lengths[0] + jnp.minimum(jnp.arange(TILE, dtype=jnp.int32) // per, drafts - 1)
+    half_dim = HEAD_DIM // 2
+    freqs = 500000.0 ** (-2.0 * jnp.arange(half_dim, dtype=F32) / HEAD_DIM)
+    angles = position.astype(F32)[:, None] * freqs
+    cosine, sine = jnp.cos(angles), jnp.sin(angles)
+    cosine = jnp.concatenate([cosine, cosine], axis=1)
+    sine = jnp.concatenate([-sine, sine], axis=1)
+    slots, kv_width = self_keys.shape[1], self_keys.shape[2]
+    images = image_keys.shape[1]
+    rows = drafts * n
+    vmem = pl.BlockSpec(memory_space=pltpu.VMEM)
+    smem = pl.BlockSpec(memory_space=pltpu.SMEM)
+    away = pl.BlockSpec(memory_space=pl.ANY)
+    out = pl.pallas_call(
+        functools.partial(layer_kernel, nz, nx, drafts),
+        out_shape=jax.ShapeDtypeStruct((drafts, model), BF16),
+        in_specs=[smem] * 3 + [vmem] * 6 + [away] * 9,
+        out_specs=vmem,
+        scratch_shapes=[
+            pltpu.VMEM(query_weight.shape, BF16),
+            pltpu.VMEM(kv_weight.shape, BF16),
+            pltpu.VMEM(out_weight.shape, BF16),
+            pltpu.VMEM(cross_query_weight.shape, BF16),
+            pltpu.VMEM(cross_out_weight.shape, BF16),
+            pltpu.VMEM((slots + LANES, kv_width), BF16),
+            pltpu.VMEM((slots + LANES, kv_width), BF16),
+            pltpu.VMEM((images, kv_width), BF16),
+            pltpu.VMEM((images, kv_width), BF16),
+            pltpu.VMEM((drafts * chunks, LANES), F32),
+            pltpu.VMEM((drafts * chunks, LANES), F32),
+            pltpu.VMEM((n * drafts * (chunks // nx), LANES), F32),
+            pltpu.VMEM((rows, model // nx), BF16),
+            pltpu.VMEM((4, drafts, chunks, LANES), BF16),
+            pltpu.VMEM((4, n, drafts, chunks // nx, LANES), BF16),
+            pltpu.VMEM((4, nx - 1, rows, width), F32),
+            pltpu.VMEM((4, nx - 1, rows, width), F32),
+            pltpu.VMEM((rows, width), F32),
+            pltpu.VMEM((n * TILE, LANES), F32),
+            pltpu.VMEM((2, n, TILE, LANES), BF16),
+            pltpu.VMEM((2, n, TILE, LANES), BF16),
+            pltpu.VMEM((4, n, TILE, LANES), F32),
+            pltpu.VMEM((n * TILE, LANES), F32),
+            pltpu.VMEM((n * TILE, LANES), BF16),
+            pltpu.SemaphoreType.DMA((9,)),
+            pltpu.SemaphoreType.DMA((4, n)),
+            pltpu.SemaphoreType.DMA((4, n)),
+            pltpu.SemaphoreType.DMA((4, nx - 1)),
+            pltpu.SemaphoreType.DMA((4, nx - 1)),
+            pltpu.SemaphoreType.DMA((4, n)),
+            pltpu.SemaphoreType.DMA((4, n)),
+        ],
+        compiler_params=pltpu.CompilerParams(
+            collective_id=0, has_side_effects=True, vmem_limit_bytes=56 * 2**20
+        ),
+        cost_estimate=pl.CostEstimate(
+            flops=2 * rows * query_weight.shape[0] * (4 * query_weight.shape[1] + kv_weight.shape[1]),
+            bytes_accessed=2 * query_weight.shape[0] * (4 * query_weight.shape[1] + kv_weight.shape[1]),
+            transcendentals=0,
+        ),
+    )(
+        cache_lengths,
+        image_counts,
+        cross_gate,
+        hidden.reshape(drafts, model),
+        norm_gain.reshape(chunks, LANES),
+        cross_norm_gain.reshape(chunks, LANES),
+        query_gain.reshape(1, HEAD_DIM),
+        cosine,
+        sine,
+        self_keys.reshape(slots, kv_width),
+        self_values.reshape(slots, kv_width),
+        image_keys.reshape(images, kv_width),
+        image_values.reshape(images, kv_width),
+        query_weight,
+        kv_weight,
+        out_weight,
+        cross_query_weight,
+        cross_out_weight,
+    )
+    return out.reshape(hidden.shape)
+
+
+def fits_kernel(hidden, kv_weight, query_weight):
+    nx = lax.axis_size("gx")
+    n = lax.axis_size("yz") * nx
+    per = query_weight.shape[1] // nx // HEAD_DIM
+    return (
+        hidden.shape[0] == 1
+        and n == 2 * KV_HEADS
+        and nx % 2 == 0
+        and query_weight.shape[1] == nx * per * HEAD_DIM
+        and per * n == HEADS
+        and kv_weight.shape[1] == nx * HEAD_DIM
+        and hidden.shape[1] * (per + 1) <= TILE
+        and query_weight.shape[0] % (TILE * LANES) == 0
+    )
+
+
+def shards(hidden, *rest):
+    if fits_kernel(hidden, rest[8], rest[7]):
+        return shards_by_kernel(hidden, *rest)
+    return shards_by_collectives(hidden, *rest)
+
+
 def solution(mesh):
     placed = (
         P(("grp", "yz", "gx"), None, None),

time: 556 us -> 92.5 us (0.17); the launches traced: 546 us -> 92.2 us
  other arithmetic: 186 us -> 0.82 us
  blocking collectives: 111 us -> 0 us
  local copies, waits for them, and re-layouts: 109 us -> 1.49 us
  Pallas kernels: 0 us -> 88 us
  waiting for transfers between devices: 79.3 us -> 0 us
  matrix products: 22.2 us -> 0 us
  starting transfers between devices: 20.8 us -> 0 us
  between operations: 16.9 us -> 1.97 us
    unnamed x4 -> x0, other arithmetic: 182 us -> none
    pallas_call x0 -> x1, Pallas kernels: none -> 88 us  [shards_by_kernel(): pl.pallas_call(functools.partial(layer_kernel, nz, nx, drafts), out_shape...]
    unnamed x4 -> x0, waiting for transfers between devices: 60.2 us -> none
    all_gather x4 -> x0, blocking collectives: 57.9 us -> none  [the longest x2 29 us: project_rows(): piece = lax.all_gather(routed, 'yz', axis=0, tiled=True)]
    unnamed x32 -> x1, local copies, waits for them, and re-layouts: 41.5 us -> 1.49 us
    all_to_all x15 -> x0, local copies, waits for them, and re-layouts: 33.3 us -> none  [the longest x6 16.6 us: rows_out(): lax.all_to_all(attended, 'gx', split_axis=2, concat_axis=0, tiled=True)]
    unnamed x2 -> x0, blocking collectives: 30.1 us -> none
    all_to_all x3 -> x0, blocking collectives: 23.5 us -> none  [the longest x2 12.8 us: rows_out(): lax.all_to_all(attended, 'gx', split_axis=2, concat_axis=0, tiled=True)]
  transfers between devices with their start and end apart: 7 -> 0, of which waited for: 7 -> 0; matrix products, arithmetic and copies ran while one was open for 1% -> 0% of each run, Pallas kernels for 0% -> 0%
where the time goes in v1:
time: 92.5 us; the launch traced here: 92.2 us
  Pallas kernels  88 us (95%)
  between operations  1.97 us (2%)
  local copies, waits for them, and re-layouts  1.49 us (2%)
    pallas_call x1, Pallas kernels, shards_by_kernel(): pl.pallas_call(functools.partial(layer_kernel, nz, nx, drafts), out_shape...  88 us

profile of v1, /device:TPU:0, one launch (start us, length us, event | category | flops | bytes accessed | tf_op | source)
XLA Modules:
  0.0 92.2 jit_solution(9559367310561658946)
XLA Ops:
  2.0 0.1 fusion
  2.1 0.7 pad_maximum_fusion
  2.8 88.0 %shard_map.154 = bf16[3,8192]{1,0:T(4,128)(2,1)} custom-call(s32[1]{0:T(128)} %copy.18.lengths_ref, s32[1]{0:T(128)S(6)} %copy.19.counts_ref, f32[1]{0:T(128)S(6)} %copy.20.gate_ref, bf16[3,8192]{1,0:T(4,128)(2,1)} %bitcast.16, f32[64,128]{1,0:T(8,128)} %bitcast.17, f32[64,128]{1,0:T(8,128)} %bitcast.18, f32[1,128]{1,0:T(1,128)} %bitcast.19, ...), custom_call_target="tpu_custom_call" | custom-call | flops 1711276032 | bytes 35651584 | tf_op jit(solution)/shard_map/pallas_call | solution.py:563
  90.7 1.5 %copy.21 = bf16[1,3,8192]{2,1,0:T(4,128)(2,1)} copy(bf16[1,3,8192]{2,1,0:T(4,128)(2,1)} %bitcast.15) | data formatting | bytes 98304
  (2 shorter events, 0.0 us)

commit v2 on v1

--- a/solution.py
+++ b/solution.py
@@ -221,7 +221,6 @@
     tile_f,
     tile_b,
     route_b,
-    route_f,
     heads_f,
     heads_b,
     load_sem,
@@ -268,7 +267,7 @@
         )
         return 0
 
-    lax.fori_loop(1, n, greet, 0)
+    lax.fori_loop(1, n, greet, 0, unroll=True)
 
     def norm_rows(rows, gain):
         scaled = []
@@ -279,6 +278,9 @@
             )
             scaled.append(x * lax.rsqrt(mean + 1e-05) * gain)
         return scaled
+
+    def far_first(k):
+        return (k + n // 2 - 2) % (n - 1) + 1
 
     def scatter_copy(stage, k, source, target):
         d = (me + k) % n
@@ -293,10 +295,11 @@
 
     def scatter(stage):
         def send(k, _):
+            k = far_first(k)
             scatter_copy(stage, k, (me + k) % n, me).start()
             return 0
 
-        lax.fori_loop(1, n, send, 0)
+        lax.fori_loop(1, n, send, 0, unroll=True)
 
     def gather(stage):
         rows = drafts * block
@@ -312,17 +315,17 @@
             ).astype(F32)
             return 0
 
-        lax.fori_loop(1, n, take, 0)
+        lax.fori_loop(1, n, take, 0, unroll=True)
         for s in range(drafts):
             for c in range(block):
                 lhs[s * n : (s + 1) * n, c * LANES : (c + 1) * LANES] = wide[
                     pl.ds(s * block + c, n, stride=rows), :
                 ].astype(BF16)
 
-    def peer(step, sign):
-        half = nx // 2
-        flip = nx - 1 - step
-        return ((i // 2 + sign * (flip // 2) + half) % half) * 2 + (i % 2 + flip % 2) % 2
+    across_chip = (1 - i // 2) * 2
+    same_chip = i // 2 * 2
+    other_core = 1 - i % 2
+    peers = (same_chip + other_core, across_chip + i % 2, same_chip + other_core)
 
     def part_copy(stage, step, width, target):
         return pltpu.make_async_remote_copy(
@@ -347,23 +350,28 @@
                 for w in weights
             ]
 
-        def send(step, _):
-            target = peer(step, 1)
+        def store(ref, target):
             at = 0
             for term in piece(target):
-                part_out[stage, step, :, at : at + term.shape[1]] = term
+                ref[:, at : at + term.shape[1]] = term
                 at += term.shape[1]
-            part_copy(stage, step, width, target).start()
-            return 0
-
-        lax.fori_loop(0, nx - 1, send, 0)
-        at = 0
-        for term in piece(i):
-            total[:, at : at + term.shape[1]] = term
-            at += term.shape[1]
-        for step in range(nx - 1):
-            part_copy(stage, step, width, peer(step, 1)).wait_recv()
-            total[:, :width] += part_in[stage, step, :, :width]
+
+        def link(step):
+            return part_copy(stage, step, width, peers[step])
+
+        store(part_out.at[stage, 0], across_chip + other_core)
+        link(0).start()
+        store(part_out.at[stage, 1], across_chip + i % 2)
+        link(0).wait_recv()
+        part_out[stage, 1, :, :width] += part_in[stage, 0, :, :width]
+        link(1).start()
+        store(part_out.at[stage, 2], peers[2])
+        link(2).start()
+        store(total, i)
+        link(2).wait_recv()
+        total[:, :width] += part_in[stage, 2, :, :width]
+        link(1).wait_recv()
+        total[:, :width] += part_in[stage, 1, :, :width]
         return width // LANES
 
     def route_copy(stage, buf_out, buf_in, k, source, target):
@@ -376,40 +384,57 @@
             device_id_type=pl.DeviceIdType.MESH,
         )
 
-    def route(stage, heads, buf_out, buf_in):
+    def route(stage, heads, finish=lambda rows: rows):
+        buf_out, buf_in = tile_b.at[stage], route_b.at[stage]
         for s in range(drafts):
             for h in range(heads):
                 tile_f[pl.ds(s * heads + h, n, stride=TILE), :] = total[
                     s * n : (s + 1) * n, h * LANES : (h + 1) * LANES
                 ]
-        buf_out[...] = tile_f[...].reshape(n, TILE, LANES).astype(buf_out.dtype)
+        buf_out[...] = finish(tile_f[...]).reshape(n, TILE, LANES).astype(BF16)
+        exchange(stage)
+        collect(stage)
+
+    def exchange(stage):
+        buf_out, buf_in = tile_b.at[stage], route_b.at[stage]
 
         def send(k, _):
+            k = far_first(k)
             route_copy(stage, buf_out, buf_in, k, (me + k) % n, me).start()
             return 0
 
-        lax.fori_loop(1, n, send, 0)
+        lax.fori_loop(1, n, send, 0, unroll=True)
         buf_in[me] = buf_out[me]
+
+    def collect(stage):
+        buf_out, buf_in = tile_b.at[stage], route_b.at[stage]
 
         def take(k, _):
             route_copy(stage, buf_out, buf_in, k, me, (me - k + n) % n).wait_recv()
             return 0
 
-        lax.fori_loop(1, n, take, 0)
+        lax.fori_loop(1, n, take, 0, unroll=True)
 
     def attend(stage, kref, vref, kv_heads, valid, heads):
         tiles = n // kv_heads
+        height = tiles * TILE
+        scores = []
         for k in range(kv_heads):
-            q = heads_b[k * tiles * TILE : (k + 1) * tiles * TILE, :]
-            lanes = slice(k * LANES, (k + 1) * LANES)
-            scores = lax.dot_general(
-                q, kref[:, lanes], (((1,), (1,)), ((), ())), preferred_element_type=F32
-            ) * LANES ** (-0.5)
-            scores = jnp.where(valid, scores, -jnp.inf)
-            weights = jnp.exp(scores - jnp.max(scores, axis=-1, keepdims=True))
-            probs = (weights / jnp.sum(weights, axis=-1, keepdims=True)).astype(BF16)
-            heads_f[k * tiles * TILE : (k + 1) * tiles * TILE, :] = jnp.dot(
-                probs, vref[:, lanes], preferred_element_type=F32
+            part = lax.dot_general(
+                heads_b[k * height : (k + 1) * height, :],
+                kref[:, k * LANES : (k + 1) * LANES],
+                (((1,), (1,)), ((), ())),
+                preferred_element_type=F32,
+            )
+            scores.append(jnp.where(valid, part * LANES ** (-0.5), -jnp.inf))
+        scores = jnp.concatenate(scores, axis=0)
+        weights = jnp.exp(scores - jnp.max(scores, axis=-1, keepdims=True))
+        probs = (weights / jnp.sum(weights, axis=-1, keepdims=True)).astype(BF16)
+        for k in range(kv_heads):
+            heads_f[k * height : (k + 1) * height, :] = jnp.dot(
+                probs[k * height : (k + 1) * height, :],
+                vref[:, k * LANES : (k + 1) * LANES],
+                preferred_element_type=F32,
             )
         for s in range(drafts):
             for d in range(n):
@@ -421,6 +446,14 @@
             wide[: drafts * chunks, :].reshape(drafts, chunks, LANES).astype(BF16)
         )
 
+    def from_tiles(stage, ref):
+        heads_f[...] = route_b[stage].reshape(n * TILE, LANES).astype(F32)
+        for s in range(drafts):
+            for d in range(n):
+                ref[s * chunks + d * per : s * chunks + (d + 1) * per, :] = heads_f[
+                    d * TILE + s * per : d * TILE + (s + 1) * per, :
+                ]
+
     for c in range(chunks):
         hid[pl.ds(c, drafts, stride=chunks), :] = hidden_ref[
             :, c * LANES : (c + 1) * LANES
@@ -430,6 +463,14 @@
     tile_f[...] = jnp.zeros_like(tile_f)
     pl.semaphore_wait(barrier, n - 1)
     scatter(0)
+    for s in range(drafts):
+        for d in range(n):
+            tile_f[d * TILE + s * per : d * TILE + (s + 1) * per, :] = hid[
+                s * chunks + d * per : s * chunks + (d + 1) * per, :
+            ]
+    tile_b[4] = tile_f[...].reshape(n, TILE, LANES).astype(BF16)
+    exchange(4)
+    tile_f[...] = jnp.zeros_like(tile_f)
     for copy in copies[2:]:
         copy.start()
     pad = keys.shape[0] - slots
@@ -440,7 +481,7 @@
     copies[0].wait()
     copies[1].wait()
     heads = project(0, (wq, wkv))
-    route(0, heads, tile_b.at[0], route_b.at[0])
+    route(0, heads)
     got = route_b[0].reshape(n * TILE, LANES).astype(F32)
     cosine = jnp.concatenate([cos_ref[...]] * n, axis=0)
     sine = jnp.concatenate([sin_ref[...]] * n, axis=0)
@@ -464,12 +505,11 @@
     copies[4].wait()
     heads = project(1, (wo,))
     tile_f[...] = jnp.zeros_like(tile_f)
-    route(1, heads, route_f.at[0], route_f.at[1])
-    for s in range(drafts):
-        for d in range(n):
-            at = s * chunks + d * per
-            mid[at : at + per, :] = hid[at : at + per, :] + route_f[1, d, s * per : (s + 1) * per, :]
-    mid[...] = mid[...].astype(BF16).astype(F32)
+    collect(4)
+    route(
+        1, heads, lambda rows: rows + route_b[4].reshape(n * TILE, LANES).astype(F32)
+    )
+    from_tiles(1, mid)
 
     for s, x in enumerate(norm_rows(mid, cross_gain_ref[...])):
         rows_out_buf[2, s] = x.astype(BF16)
@@ -477,8 +517,8 @@
     gather(2)
     copies[5].wait()
     heads = project(2, (wcq,))
-    route(2, heads, tile_b.at[1], route_b.at[1])
-    got = route_b[1].reshape(n * TILE, LANES).astype(F32)
+    route(2, heads)
+    got = route_b[2].reshape(n * TILE, LANES).astype(F32)
     scale = lax.rsqrt(jnp.mean(got * got, axis=-1, keepdims=True) + 1e-05)
     heads_b[...] = (got * scale * query_gain_ref[...]).astype(BF16)
     copies[6].wait()
@@ -490,36 +530,34 @@
     gather(3)
     copies[8].wait()
     heads = project(3, (wco,))
-    route(3, heads, route_f.at[2], route_f.at[3])
     gate = jnp.tanh(jnp.full((1, LANES), gate_ref[0], F32))
-    for s in range(drafts):
-        for d in range(n):
-            at = s * chunks + d * per
-            wide[at : at + per, :] = (
-                mid[at : at + per, :] + gate * route_f[3, d, s * per : (s + 1) * per, :]
-            )
+    route(
+        3,
+        heads,
+        lambda rows: tile_b[1].reshape(n * TILE, LANES).astype(F32) + gate * rows,
+    )
+    from_tiles(3, mid)
     for c in range(chunks):
-        out_ref[:, c * LANES : (c + 1) * LANES] = wide[
+        out_ref[:, c * LANES : (c + 1) * LANES] = mid[
             pl.ds(c, drafts, stride=chunks), :
         ].astype(BF16)
 
+    def gone(k, _):
+        route_copy(4, tile_b.at[4], route_b.at[4], k, me, me).wait_send()
+        return 0
+
+    lax.fori_loop(1, n, gone, 0)
     for stage in range(4):
 
         def sent(k, _):
             scatter_copy(stage, k, me, me).wait_send()
-            out_buf, in_buf = [
-                (tile_b.at[0], route_b.at[0]),
-                (route_f.at[0], route_f.at[1]),
-                (tile_b.at[1], route_b.at[1]),
-                (route_f.at[2], route_f.at[3]),
-            ][stage]
-            route_copy(stage, out_buf, in_buf, k, me, me).wait_send()
+            route_copy(stage, tile_b.at[stage], route_b.at[stage], k, me, me).wait_send()
             return 0
 
         lax.fori_loop(1, n, sent, 0)
         width = total.shape[1] if stage == 0 else cols
         for step in range(nx - 1):
-            part_copy(stage, step, width, peer(step, 1)).wait_send()
+            part_copy(stage, step, width, peers[step]).wait_send()
 
 
 def shards_by_kernel(
@@ -585,9 +623,8 @@
             pltpu.VMEM((4, nx - 1, rows, width), F32),
             pltpu.VMEM((rows, width), F32),
             pltpu.VMEM((n * TILE, LANES), F32),
-            pltpu.VMEM((2, n, TILE, LANES), BF16),
-            pltpu.VMEM((2, n, TILE, LANES), BF16),
-            pltpu.VMEM((4, n, TILE, LANES), F32),
+            pltpu.VMEM((5, n, TILE, LANES), BF16),
+            pltpu.VMEM((5, n, TILE, LANES), BF16),
             pltpu.VMEM((n * TILE, LANES), F32),
             pltpu.VMEM((n * TILE, LANES), BF16),
             pltpu.SemaphoreType.DMA((9,)),
@@ -595,8 +632,8 @@
             pltpu.SemaphoreType.DMA((4, n)),
             pltpu.SemaphoreType.DMA((4, nx - 1)),
             pltpu.SemaphoreType.DMA((4, nx - 1)),
-            pltpu.SemaphoreType.DMA((4, n)),
-            pltpu.SemaphoreType.DMA((4, n)),
+            pltpu.SemaphoreType.DMA((5, n)),
+            pltpu.SemaphoreType.DMA((5, n)),
         ],
         compiler_params=pltpu.CompilerParams(
             collective_id=0, has_side_effects=True, vmem_limit_bytes=56 * 2**20
@@ -636,7 +673,7 @@
     return (
         hidden.shape[0] == 1
         and n == 2 * KV_HEADS
-        and nx % 2 == 0
+        and nx == 4
         and query_weight.shape[1] == nx * per * HEAD_DIM
         and per * n == HEADS
         and kv_weight.shape[1] == nx * HEAD_DIM

time: 92.5 us -> 84 us (0.908)
  Pallas kernels: 88 us -> 79.5 us
    pallas_call x1, Pallas kernels: 88 us -> 79.5 us  [shards_by_kernel(): pl.pallas_call(functools.partial(layer_kernel, nz, nx, drafts), out_shape...]
where the time goes in v2:
time: 84 us; the launch traced here: 83.8 us
  Pallas kernels  79.5 us (95%)
  between operations  1.97 us (2%)
  local copies, waits for them, and re-layouts  1.49 us (2%)
    pallas_call x1, Pallas kernels, shards_by_kernel(): pl.pallas_call(functools.partial(layer_kernel, nz, nx, drafts), out_shape...  79.5 us

profile of v2, /device:TPU:0, one launch (start us, length us, event | category | flops | bytes accessed | tf_op | source)
XLA Modules:
  0.0 83.8 jit_solution(5573696740514291567)
XLA Ops:
  2.0 0.1 fusion
  2.1 0.7 pad_maximum_fusion
  2.8 79.5 %shard_map.154 = bf16[3,8192]{1,0:T(4,128)(2,1)} custom-call(s32[1]{0:T(128)} %copy.18.lengths_ref, s32[1]{0:T(128)S(6)} %copy.19.counts_ref, f32[1]{0:T(128)S(6)} %copy.20.gate_ref, bf16[3,8192]{1,0:T(4,128)(2,1)} %bitcast.16, f32[64,128]{1,0:T(8,128)} %bitcast.17, f32[64,128]{1,0:T(8,128)} %bitcast.18, f32[1,128]{1,0:T(1,128)} %bitcast.19, ...), custom_call_target="tpu_custom_call" | custom-call | flops 1711276032 | bytes 35651584 | tf_op jit(solution)/shard_map/pallas_call | solution.py:601
  82.3 1.5 %copy.21 = bf16[1,3,8192]{2,1,0:T(4,128)(2,1)} copy(bf16[1,3,8192]{2,1,0:T(4,128)(2,1)} %bitcast.15) | data formatting | bytes 98304
  (2 shorter events, 0.0 us)

commit v3 on v2

--- a/solution.py
+++ b/solution.py
@@ -287,8 +287,8 @@
         return pltpu.make_async_remote_copy(
             src_ref=rows_out_buf.at[stage, :, pl.ds(pl.multiple_of((source % nx) * block, block), block)],
             dst_ref=rows_in.at[stage, target],
-            send_sem=scat_send.at[stage, k],
-            recv_sem=scat_recv.at[stage, k],
+            send_sem=scat_send.at[stage],
+            recv_sem=scat_recv.at[stage],
             device_id=place(d),
             device_id_type=pl.DeviceIdType.MESH,
         )
@@ -301,21 +301,30 @@
 
         lax.fori_loop(1, n, send, 0, unroll=True)
 
+    def all_rows(stage, sems):
+        every = rows_in.at[stage, pl.ds(0, n - 1)]
+        pltpu.make_async_copy(every, every, sems.at[stage]).wait()
+
+    def all_tiles(stage, sems):
+        every = route_b.at[stage, pl.ds(0, n - 1)]
+        pltpu.make_async_copy(every, every, sems.at[stage]).wait()
+
     def gather(stage):
         rows = drafts * block
         own = rows_out_buf[stage, :, pl.ds(pl.multiple_of(i * block, block), block), :]
         wide[pl.ds(pl.multiple_of(me * rows, TILE), rows), :] = own.reshape(rows, LANES).astype(F32)
 
-        def take(k, _):
+        all_rows(stage, scat_recv)
+
+        def widen(k, _):
             source = (me - k + n) % n
-            scatter_copy(stage, k, me, source).wait_recv()
             got = rows_in[stage, source]
             wide[pl.ds(pl.multiple_of(source * rows, TILE), rows), :] = got.reshape(
                 rows, LANES
             ).astype(F32)
             return 0
 
-        lax.fori_loop(1, n, take, 0, unroll=True)
+        lax.fori_loop(1, n, widen, 0, unroll=True)
         for s in range(drafts):
             for c in range(block):
                 lhs[s * n : (s + 1) * n, c * LANES : (c + 1) * LANES] = wide[
@@ -378,8 +387,8 @@
         return pltpu.make_async_remote_copy(
             src_ref=buf_out.at[source],
             dst_ref=buf_in.at[target],
-            send_sem=route_send.at[stage, k],
-            recv_sem=route_recv.at[stage, k],
+            send_sem=route_send.at[stage],
+            recv_sem=route_recv.at[stage],
             device_id=place((me + k) % n),
             device_id_type=pl.DeviceIdType.MESH,
         )
@@ -407,13 +416,7 @@
         buf_in[me] = buf_out[me]
 
     def collect(stage):
-        buf_out, buf_in = tile_b.at[stage], route_b.at[stage]
-
-        def take(k, _):
-            route_copy(stage, buf_out, buf_in, k, me, (me - k + n) % n).wait_recv()
-            return 0
-
-        lax.fori_loop(1, n, take, 0, unroll=True)
+        all_tiles(stage, route_recv)
 
     def attend(stage, kref, vref, kv_heads, valid, heads):
         tiles = n // kv_heads
@@ -542,19 +545,10 @@
             pl.ds(c, drafts, stride=chunks), :
         ].astype(BF16)
 
-    def gone(k, _):
-        route_copy(4, tile_b.at[4], route_b.at[4], k, me, me).wait_send()
-        return 0
-
-    lax.fori_loop(1, n, gone, 0)
+    all_tiles(4, route_send)
     for stage in range(4):
-
-        def sent(k, _):
-            scatter_copy(stage, k, me, me).wait_send()
-            route_copy(stage, tile_b.at[stage], route_b.at[stage], k, me, me).wait_send()
-            return 0
-
-        lax.fori_loop(1, n, sent, 0)
+        all_rows(stage, scat_send)
+        all_tiles(stage, route_send)
         width = total.shape[1] if stage == 0 else cols
         for step in range(nx - 1):
             part_copy(stage, step, width, peers[step]).wait_send()
@@ -628,12 +622,12 @@
             pltpu.VMEM((n * TILE, LANES), F32),
             pltpu.VMEM((n * TILE, LANES), BF16),
             pltpu.SemaphoreType.DMA((9,)),
-            pltpu.SemaphoreType.DMA((4, n)),
-            pltpu.SemaphoreType.DMA((4, n)),
+            pltpu.SemaphoreType.DMA((4,)),
+            pltpu.SemaphoreType.DMA((4,)),
             pltpu.SemaphoreType.DMA((4, nx - 1)),
             pltpu.SemaphoreType.DMA((4, nx - 1)),
-            pltpu.SemaphoreType.DMA((5, n)),
-            pltpu.SemaphoreType.DMA((5, n)),
+            pltpu.SemaphoreType.DMA((5,)),
+            pltpu.SemaphoreType.DMA((5,)),
         ],
         compiler_params=pltpu.CompilerParams(
             collective_id=0, has_side_effects=True, vmem_limit_bytes=56 * 2**20

time: 84 us -> 80.9 us (0.963)
  Pallas kernels: 79.5 us -> 76.4 us
    pallas_call x1, Pallas kernels: 79.5 us -> 76.4 us  [shards_by_kernel(): pl.pallas_call(functools.partial(layer_kernel, nz, nx, drafts), out_shape...]
where the time goes in v3:
time: 80.9 us; the launch traced here: 80.6 us
  Pallas kernels  76.4 us (94%)
  between operations  1.97 us (2%)
  local copies, waits for them, and re-layouts  1.49 us (2%)
  other arithmetic  0.82 us (1%)
    pallas_call x1, Pallas kernels, shards_by_kernel(): pl.pallas_call(functools.partial(layer_kernel, nz, nx, drafts), out_shape...  76.4 us

profile of v3, /device:TPU:0, one launch (start us, length us, event | category | flops | bytes accessed | tf_op | source)
XLA Modules:
  0.0 80.6 jit_solution(2014455368861465984)
XLA Ops:
  2.0 0.1 fusion
  2.1 0.7 pad_maximum_fusion
  2.8 76.4 %shard_map.154 = bf16[3,8192]{1,0:T(4,128)(2,1)} custom-call(s32[1]{0:T(128)} %copy.18.lengths_ref, s32[1]{0:T(128)S(6)} %copy.19.counts_ref, f32[1]{0:T(128)S(6)} %copy.20.gate_ref, bf16[3,8192]{1,0:T(4,128)(2,1)} %bitcast.16, f32[64,128]{1,0:T(8,128)} %bitcast.17, f32[64,128]{1,0:T(8,128)} %bitcast.18, f32[1,128]{1,0:T(1,128)} %bitcast.19, ...), custom_call_target="tpu_custom_call" | custom-call | flops 1711276032 | bytes 35651584 | tf_op jit(solution)/shard_map/pallas_call | solution.py:595
  79.2 1.5 %copy.21 = bf16[1,3,8192]{2,1,0:T(4,128)(2,1)} copy(bf16[1,3,8192]{2,1,0:T(4,128)(2,1)} %bitcast.15) | data formatting | bytes 98304
  (2 shorter events, 0.0 us)
